TPU v7x, 256 devices: a whole 4x4x8 slice. The times are simulated.
256 devices in a mesh: seq: 16 (over z, core), head: 4 (over x), dp: 4 (over y).
Axes of the slice: x: 4, y: 4, z: 8, core: 2. Of those that a mesh axis runs over, the one named last changes fastest.
Arguments:
- self_queries: bfloat16 [4, 2048, 2560], P('dp', ('seq', 'head')), may hold values from -8 to 8
- self_keys: bfloat16 [4, 2048, 2560], P('dp', ('seq', 'head')), may hold values from -4 to 4
- self_values: bfloat16 [4, 2048, 2560], P('dp', ('seq', 'head')), may hold values from -6 to 6
- self_cotangent: bfloat16 [4, 2048, 2560], P('dp', ('seq', 'head')), may hold values from -6 to 6
- text_queries: bfloat16 [4, 4096, 2560], P('dp', 'seq', 'head'), may hold values from -8 to 8
- memory_keys: bfloat16 [4, 2048, 2560], P('dp', 'seq', 'head'), may hold values from -4 to 4
- memory_values: bfloat16 [4, 2048, 2560], P('dp', 'seq', 'head'), may hold values from -6 to 6
- text_cotangent: bfloat16 [4, 4096, 2560], P('dp', 'seq', 'head'), may hold values from -6 to 6
- slopes: float32 [2, 20], P(None, 'head'), may hold values from 0.01 to 0.3
- page_counts: int32 [4, 4], P('dp'), may hold values from 1 to 1024, as said below
- page_cols: int32 [4, 4], P('dp'), may hold values from 4 to 64
- text_page: int32 [4, 4096], P('dp'), may hold values from 0 to 3, as said below
Outputs:
- self_query_grad: bfloat16 [4, 2048, 2560], P('dp', ('seq', 'head'))
- self_key_grad: bfloat16 [4, 2048, 2560], P('dp', ('seq', 'head'))
- self_value_grad: bfloat16 [4, 2048, 2560], P('dp', ('seq', 'head'))
- slope_grad: float32 [2, 20], P(None, 'head')
- text_query_grad: bfloat16 [4, 4096, 2560], P('dp', 'seq', 'head')
- memory_key_grad: bfloat16 [4, 2048, 2560], P('dp', 'seq', 'head')
- memory_value_grad: bfloat16 [4, 2048, 2560], P('dp', 'seq', 'head')
Inputs may be any that keep to these rules, and one draw needn't show every extreme that they name: `page_counts`: each pack's counts sum to 2048; one page of every pack has exactly 1024 patches. `text_page`: never falls along a pack's text rows; every page has at least one text row.
All inputs are finite; a program needn't handle non-finite values.
Results may differ from a plain program's by a relative error of at most 0.006.
Values may be sent and summed in bfloat16 or wider, within the bound.
No kernel may reach another device: no remote copies, remote signals or barrier semaphores. Data moves between devices by JAX's collectives and lax.ppermute only.
A program may use at most 128 MiB of HBM per device.

v0:
```python
import jax
import jax.numpy as jnp
from jax import lax
from jax.sharding import PartitionSpec as P

MASK_FILL = -1e30


def page_layout(counts, widths, patch_total):
    page_ends = jnp.cumsum(counts)
    starts = page_ends - counts
    positions = jnp.arange(patch_total, dtype=jnp.int32)
    page_ids = jnp.sum((positions[:, None] >= page_ends[None, :]).astype(jnp.int32), axis=1)
    one_hot = page_ids[:, None] == jnp.arange(counts.shape[0], dtype=jnp.int32)[None, :]
    page_start = jnp.sum(jnp.where(one_hot, starts[None, :], 0), axis=1)
    page_width = jnp.sum(jnp.where(one_hot, widths[None, :], 0), axis=1)
    offsets = positions - page_start
    return (page_ids, offsets // page_width, offsets % page_width)


def take_rows(vector, row_start, row_count):
    return lax.dynamic_slice_in_dim(vector, row_start, row_count, 0)


def heads_of(matrix, head_count):
    return matrix.reshape(matrix.shape[0], head_count, -1)


def alibi(slopes, query_layout, key_layout):
    row_gap = jnp.abs(query_layout[1][:, None] - key_layout[1][None, :]).astype(jnp.float32)
    col_gap = jnp.abs(query_layout[2][:, None] - key_layout[2][None, :]).astype(jnp.float32)
    same_page = query_layout[0][:, None] == key_layout[0][None, :]
    decay = -(slopes[0][:, None, None] * row_gap[None] + slopes[1][:, None, None] * col_gap[None])
    return (jnp.where(same_page[None], decay, MASK_FILL), row_gap, col_gap)


def query_side(queries, key_rows, value_rows, grad_rows, logit_bias):
    inv_root = queries.shape[2] ** (-0.5)
    scores = (
        jnp.einsum("rhs,khs->hrk", queries, key_rows, preferred_element_type=jnp.float32) * inv_root
        + logit_bias
    )
    row_max = jnp.max(scores, axis=2, keepdims=True)
    weights = jnp.exp(scores - row_max)
    row_total = jnp.sum(weights, axis=2, keepdims=True)
    softmax_w = weights / row_total
    log_total = (row_max + jnp.log(row_total))[:, :, 0]
    grad_probs = jnp.einsum(
        "rhs,khs->hrk", grad_rows, value_rows, preferred_element_type=jnp.float32
    )
    row_delta = jnp.sum(softmax_w * grad_probs, axis=2, keepdims=True)
    grad_scores = softmax_w * (grad_probs - row_delta)
    grad_scores_b = grad_scores.astype(jnp.bfloat16)
    query_grad = (
        jnp.einsum("hrk,khs->rhs", grad_scores_b, key_rows, preferred_element_type=jnp.float32)
        * inv_root
    )
    return (
        query_grad,
        grad_scores,
        grad_scores_b,
        softmax_w.astype(jnp.bfloat16),
        log_total,
        row_delta[:, :, 0],
    )


def key_terms(grad_scores_b, softmax_b, queries, grad_rows, row_count):
    inv_root = queries.shape[3] ** (-0.5)
    key_grad = (
        jnp.einsum("chrk,crhs->khs", grad_scores_b, queries, preferred_element_type=jnp.float32)
        * inv_root
    )
    value_grad = jnp.einsum(
        "chrk,crhs->khs", softmax_b, grad_rows, preferred_element_type=jnp.float32
    )
    return jnp.stack([key_grad.reshape(row_count, -1), value_grad.reshape(row_count, -1)], axis=1)


def local(
    self_queries,
    self_keys,
    self_values,
    self_cotangent,
    text_queries,
    memory_keys,
    memory_values,
    text_cotangent,
    slopes,
    page_counts,
    page_cols,
    text_page,
):
    head_count = slopes.shape[1]
    regrouped = (
        lax.all_to_all(self_queries[0], "head", split_axis=1, concat_axis=0, tiled=True),
        lax.all_to_all(self_keys[0], "head", split_axis=1, concat_axis=0, tiled=True),
        lax.all_to_all(self_values[0], "head", split_axis=1, concat_axis=0, tiled=True),
        lax.all_to_all(self_cotangent[0], "head", split_axis=1, concat_axis=0, tiled=True),
    )
    local_queries, local_keys, local_values, local_grads = regrouped
    patch_rows = local_queries.shape[0]
    all_keys, all_values = (
        lax.all_gather(local_keys, "seq", axis=0, tiled=True),
        lax.all_gather(local_values, "seq", axis=0, tiled=True),
    )
    patch_total = all_keys.shape[0]
    whole_layout = page_layout(page_counts[0], page_cols[0], patch_total)
    own_start = lax.axis_index("seq") * patch_rows
    own_layout = tuple((take_rows(item, own_start, patch_rows) for item in whole_layout))
    self_bias, row_gap, col_gap = alibi(slopes, own_layout, whole_layout)
    query_heads = heads_of(local_queries, head_count)
    grad_heads = heads_of(local_grads, head_count)
    self_dq, self_ds, self_ds_b, self_p_b, self_lse, self_delta = query_side(
        query_heads,
        heads_of(all_keys, head_count),
        heads_of(all_values, head_count),
        grad_heads,
        self_bias,
    )
    slope_local = -jnp.stack(
        [
            jnp.sum(self_ds * row_gap[None], axis=(1, 2)),
            jnp.sum(self_ds * col_gap[None], axis=(1, 2)),
        ]
    )
    self_ds_blocks = self_ds_b[None]
    self_p_blocks = self_p_b[None]
    query_blocks = query_heads[None]
    grad_blocks = grad_heads[None]
    self_pair = lax.psum_scatter(
        key_terms(
            self_ds_blocks,
            self_p_blocks,
            query_blocks,
            grad_blocks,
            patch_rows * lax.axis_size("seq"),
        ),
        "seq",
        scatter_dimension=0,
        tiled=True,
    )
    self_dk = self_pair[:, 0]
    self_dv = self_pair[:, 1]
    restored = (
        lax.all_to_all(
            self_dq.reshape(patch_rows, -1).astype(jnp.bfloat16),
            "head",
            split_axis=0,
            concat_axis=1,
            tiled=True,
        ),
        lax.all_to_all(
            self_dk.astype(jnp.bfloat16), "head", split_axis=0, concat_axis=1, tiled=True
        ),
        lax.all_to_all(
            self_dv.astype(jnp.bfloat16), "head", split_axis=0, concat_axis=1, tiled=True
        ),
    )
    slope_grad = lax.psum(slope_local, ("seq", "dp")) / patch_total
    memory_all_keys, memory_all_values = (
        lax.all_gather(memory_keys[0], "seq", axis=0, tiled=True),
        lax.all_gather(memory_values[0], "seq", axis=0, tiled=True),
    )
    memory_all_key_heads = heads_of(memory_all_keys, head_count)
    memory_all_value_heads = heads_of(memory_all_values, head_count)
    text_rows = text_queries.shape[1]
    text_start = lax.axis_index("seq") * text_rows
    text_ids = text_page[0]
    own_text = take_rows(text_ids, text_start, text_rows)
    text_query_heads = heads_of(text_queries[0], head_count)
    text_grad_heads = heads_of(text_cotangent[0], head_count)
    block_count = text_rows // text_rows
    text_query_blocks = text_query_heads.reshape(block_count, text_rows, head_count, -1)
    text_grad_blocks = text_grad_heads.reshape(block_count, text_rows, head_count, -1)

    def cross_block(inputs):
        block_queries, block_grads, block_pages = inputs
        block_bias = jnp.where(
            block_pages[:, None] == whole_layout[0][None, :], 0.0, MASK_FILL
        ).astype(jnp.float32)[None]
        result = query_side(
            block_queries, memory_all_key_heads, memory_all_value_heads, block_grads, block_bias
        )
        return (result[0], result[2], result[3], result[4], result[5])

    cross_out = lax.map(
        cross_block, (text_query_blocks, text_grad_blocks, own_text.reshape(block_count, text_rows))
    )
    text_dq = cross_out[0].reshape(text_rows, -1)
    text_ds_b = cross_out[1]
    text_p_b = cross_out[2]
    memory_pair = lax.psum_scatter(
        key_terms(
            text_ds_b,
            text_p_b,
            text_query_blocks,
            text_grad_blocks,
            patch_rows * lax.axis_size("seq"),
        ),
        "seq",
        scatter_dimension=0,
        tiled=True,
    )
    memory_dk = memory_pair[:, 0]
    memory_dv = memory_pair[:, 1]
    return (
        restored[0][None],
        restored[1][None],
        restored[2][None],
        slope_grad,
        text_dq.astype(jnp.bfloat16)[None],
        memory_dk.astype(jnp.bfloat16)[None],
        memory_dv.astype(jnp.bfloat16)[None],
    )


def solution(mesh):
    in_specs = (
        P("dp", ("seq", "head"), None),
        P("dp", ("seq", "head"), None),
        P("dp", ("seq", "head"), None),
        P("dp", ("seq", "head"), None),
        P("dp", "seq", "head"),
        P("dp", "seq", "head"),
        P("dp", "seq", "head"),
        P("dp", "seq", "head"),
        P(None, "head"),
        P("dp", None),
        P("dp", None),
        P("dp", None),
    )
    out_specs = (
        P("dp", ("seq", "head"), None),
        P("dp", ("seq", "head"), None),
        P("dp", ("seq", "head"), None),
        P(None, "head"),
        P("dp", "seq", "head"),
        P("dp", "seq", "head"),
        P("dp", "seq", "head"),
    )
    return jax.shard_map(local, mesh=mesh, in_specs=in_specs, out_specs=out_specs, check_vma=False)
```

profile of v0, /device:TPU:2, one launch (start us, length us, event | category | flops | bytes accessed | tf_op | source)
XLA Modules:
  0.0 406.0 jit_solution(9305916653580052399)
XLA Ops:
  7.3 1.0 all_to_all.85
  8.3 10.0 %all_to_all.109 = bf16[32,4,640]{2,0,1:T(8,128)(2,1)} all-to-all(bf16[32,4,640]{2,0,1:T(8,128)(2,1)S(1)} %copy.117), channel_id=1, replica_groups=mesh['seq'=16,'head'=4,'dp'=4] {'head'}, dimensions={1} | all-to-all | bytes 327680 | tf_op jit(solution)/shard_map/all_to_all | solution.py:97
  18.4 1.0 all_to_all.92
  19.4 9.2 %all_to_all.110 = bf16[32,4,640]{2,0,1:T(8,128)(2,1)} all-to-all(bf16[32,4,640]{2,0,1:T(8,128)(2,1)S(1)} %copy.122), channel_id=1, replica_groups=mesh['seq'=16,'head'=4,'dp'=4] {'head'}, dimensions={1} | all-to-all | bytes 327680 | tf_op jit(solution)/shard_map/all_to_all | solution.py:98
  28.6 1.7 copy.136
  30.4 1.0 all_to_all.82
  31.4 0.7 copy.116
  32.1 4.7 %all-to-all-start = ((bf16[32,4,640]{2,0,1:T(8,128)(2,1)}), bf16[32,4,640]{2,0,1:T(8,128)(2,1)S(1)}, u32[]{:S(2)}, u32[]{:S(2)}) async-start(bf16[32,4,640]{2,0,1:T(8,128)(2,1)} %copy.116), calls=%async_computation | async-start | bytes 327680 | tf_op jit(solution)/shard_map/all_to_all | solution.py:96
  36.8 1.7 copy.140
  38.6 0.8 reduce-window.4
  39.4 0.7 fusion.25
  40.2 0.8 select_reduce_fusion.1
  41.4 1.8 abs_convert_fusion
  43.5 0.7 copy.121
  44.2 4.8 %all-to-all-start.2 = ((bf16[32,4,640]{2,0,1:T(8,128)(2,1)}), bf16[32,4,640]{2,0,1:T(8,128)(2,1)S(1)}, u32[]{:S(2)}, u32[]{:S(2)}) async-start(bf16[32,4,640]{2,0,1:T(8,128)(2,1)} %copy.121), calls=%async_computation.2 | async-start | bytes 327680 | tf_op jit(solution)/shard_map/all_to_all | solution.py:99
  49.4 4.3 %all-to-all-done.2 = bf16[32,4,640]{2,0,1:T(8,128)(2,1)S(1)} async-done(((bf16[32,4,640]{2,0,1:T(8,128)(2,1)}), bf16[32,4,640]{2,0,1:T(8,128)(2,1)S(1)}, u32[]{:S(2)}, u32[]{:S(2)}) %all-to-all-start.2) | async-done | bytes 163872 | tf_op jit(solution)/shard_map/all_to_all | solution.py:99
  54.1 6.2 %all-gather.7.cloned.1.call-done = bf16[2048,640]{1,0:T(8,128)(2,1)} async-done(((bf16[128,640]{1,0:T(8,128)(2,1)}), bf16[2048,640]{1,0:T(8,128)(2,1)}) %all-gather.7.cloned.1.call-update) | async-done | bytes 2621456 | tf_op jit(solution)/shard_map/all_gather | solution.py:104
  60.3 3.0 copy.118
  63.3 37.8 %all-gather.9.cloned.1.call-done = bf16[2048,640]{1,0:T(8,128)(2,1)} async-done(((bf16[128,640]{1,0:T(8,128)(2,1)}), bf16[2048,640]{1,0:T(8,128)(2,1)}) %all-gather.9.cloned.1.call-update) | async-done | bytes 2621456 | tf_op jit(solution)/shard_map/all_gather | solution.py:105
  101.0 4.5 %copy.123 = bf16[2048,640]{0,1:T(8,128)(2,1)} copy(bf16[2048,640]{1,0:T(8,128)(2,1)} %all-gather.9.cloned.1.call-done) | data formatting | bytes 5242880 | tf_op jit(solution)/shard_map/all_gather | solution.py:105
  105.5 3.6 select_add_fusion
  109.1 1.6 fusion.28
  110.7 1.0 copy-done.4
  111.7 1.0 copy-done.7
  112.7 1.3 multiply_reduce_fusion.3
  114.3 2.4 multiply_reduce_fusion.2
  116.7 3.2 convolution_multiply_fusion
  119.8 6.0 %copy.131 = f32[2048,1,640]{2,0,1:T(8,128)} copy(f32[2048,1,640]{0,2,1:T(8,128)} %bitcast.79) | data formatting | bytes 10485760 | tf_op jit(solution)/shard_map/stack;reshape | solution.py:77
  125.8 8.0 %fusion.7 = f32[5,2048,128]{1,2,0:T(8,128)} fusion(bf16[128,5,128]{0,2,1:T(8,128)(2,1)S(1)} %copy.130, f32[5,128]{1,0:T(8,128)S(1)} %get-tuple-element.85, f32[5,128,2048]{2,1,0:T(8,128)} %copy-done.4), kind=kOutput, calls=%fused_computation.22 | convolution fusion | flops 339479168 | bytes 10652160 | tf_op jit(solution)/shard_map/chrk,crhs->khs/dot_general | solution.py:74
  133.7 5.9 %copy.132 = f32[2048,1,640]{2,0,1:T(8,128)} copy(f32[2048,1,640]{0,2,1:T(8,128)} %bitcast.84) | data formatting | bytes 10485760 | tf_op jit(solution)/shard_map/stack;reshape | solution.py:77
  139.6 8.8 %pad_maximum_fusion = f32[2048,2,640]{2,0,1:T(8,128)} fusion(f32[2048,1,640]{2,0,1:T(8,128)} %copy.132, f32[2048,1,640]{2,0,1:T(8,128)} %copy.131), kind=kLoop, calls=%fused_computation.2 | loop fusion | flops 2621440 | bytes 20971520 | tf_op jit(solution)/shard_map/stack | solution.py:77
  148.7 0.7 copy-done.8
  149.6 1.1 copy.139
  150.8 1.6 compare_select_fusion
  152.4 9.5 %fusion.29 = (f32[5,256]{1,0:T(8,128)S(1)}, f32[5,256,2048]{2,1,0:T(8,128)}) fusion(f32[256,2048]{1,0:T(8,128)} %compare_select_fusion, bf16[256,5,128]{0,2,1:T(8,128)(2,1)S(1)} %bitcast.87, bf16[2048,5,128]{0,2,1:T(8,128)(2,1)} %bitcast.104), kind=kOutput, calls=%fused_computation.62 | convolution fusion | flops 681576448 | bytes 15537152 | tf_op jit(solution)/shard_map/while/body/eval_jaxpr/sub | solution.py:44
  161.8 27.1 %all-gather.13.cloned.1.call-done = bf16[1,2048,640]{1,2,0:T(8,128)(2,1)} async-done(((bf16[1,128,640]{1,2,0:T(8,128)(2,1)}), bf16[1,2048,640]{1,2,0:T(8,128)(2,1)}) %all-gather.13.cloned.1.call-update) | async-done | bytes 2621456 | tf_op jit(solution)/shard_map/all_gather | solution.py:163
  189.0 6.1 %multiply_reduce_fusion = (f32[5,256]{1,0:T(8,128)S(1)}, f32[5,256,2048]{2,1,0:T(8,128)S(1)}) fusion(f32[5,256,2048]{2,1,0:T(8,128)} %get-tuple-element.90, f32[5,256]{1,0:T(8,128)S(1)} %get-tuple-element.89, bf16[256,5,128]{0,2,1:T(8,128)(2,1)S(1)} %bitcast.96, bf16[2048,5,128]{0,2,1:T(8,128)(2,1)} %bitcast.106), kind=kOutput, calls=%fused_computation.5 | convolution fusion | flops 678951680 | bytes 23930880 | tf_op jit(solution)/shard_map/while/body/eval_jaxpr/rhs,khs->hrk/dot_general | solution.py:48
  195.1 1.1 slice-done.1
  196.2 0.6 slice-done.2
  196.8 1.8 multiply_convert_fusion
  198.6 3.9 convolution_multiply_fusion.1
  202.6 5.9 %copy.143 = f32[2048,1,640]{2,0,1:T(8,128)} copy(f32[2048,1,640]{0,2,1:T(8,128)} %bitcast.78) | data formatting | bytes 10485760 | tf_op jit(solution)/shard_map/stack;reshape | solution.py:77
  208.5 7.4 %fusion.3 = f32[5,2048,128]{1,2,0:T(8,128)} fusion(bf16[256,5,128]{0,2,1:T(8,128)(2,1)S(1)} %bitcast.97, f32[5,256,2048]{2,1,0:T(8,128)} %get-tuple-element.90, f32[5,256]{1,0:T(8,128)S(1)} %get-tuple-element.89), kind=kOutput, calls=%fused_computation.9 | convolution fusion | flops 676331520 | bytes 16061440 | tf_op jit(solution)/shard_map/chrk,crhs->khs/dot_general | solution.py:74
  215.9 5.9 %copy.144 = f32[2048,1,640]{2,0,1:T(8,128)} copy(f32[2048,1,640]{0,2,1:T(8,128)} %bitcast.85) | data formatting | bytes 10485760 | tf_op jit(solution)/shard_map/stack;reshape | solution.py:77
  221.9 8.7 %pad_maximum_fusion.1 = f32[2048,2,640]{2,0,1:T(8,128)} fusion(f32[2048,1,640]{2,0,1:T(8,128)} %copy.144, f32[2048,1,640]{2,0,1:T(8,128)} %copy.143), kind=kLoop, calls=%fused_computation.3 | loop fusion | flops 2621440 | bytes 20971520 | tf_op jit(solution)/shard_map/stack | solution.py:77
  230.6 5.3 %fusion.14 = bf16[5,256,128]{1,2,0:T(8,128)(2,1)S(1)} fusion(bf16[5,256,2048]{2,1,0:T(8,128)(2,1)} %copy-done.2, bf16[2048,5,128]{0,2,1:T(8,128)(2,1)} %bitcast.105), kind=kOutput, calls=%fused_computation.31 | convolution fusion | flops 671416320 | bytes 8192000 | tf_op jit(solution)/shard_map/while/body/eval_jaxpr/hrk,khs->rhs/dot_general | solution.py:55
  236.0 0.9 copy.145
  236.9 129.5 %psum.7 = f32[2,5]{1,0:T(2,128)S(1)} all-reduce(f32[2,5]{1,0:T(2,128)S(1)} %maximum_negate_fusion), channel_id=1, replica_groups=mesh['seq'=16,'head'=4,'dp'=4] {'seq','dp'}, use_global_device_ids=true, to_apply=%region_10.11 | all-reduce | flops 10 | bytes 80 | tf_op jit(solution)/shard_map/psum | solution.py:160
  366.3 2.6 fusion.21
  369.0 0.9 convert_element_type.95
  369.9 4.8 %all-to-all-start.4 = ((bf16[4,32,640]{2,1,0:T(8,128)(2,1)}), bf16[4,32,640]{2,1,0:T(8,128)(2,1)S(1)}, u32[]{:S(2)}, u32[]{:S(2)}) async-start(bf16[4,32,640]{2,1,0:T(8,128)(2,1)} %convert_element_type.95), calls=%async_computation.4 | async-start | bytes 327680 | tf_op jit(solution)/shard_map/all_to_all | solution.py:146
  374.7 1.1 convert.8
  375.8 0.8 fusion.27
  376.6 2.8 all-to-all-done.4
  379.4 4.8 %all-to-all-start.5 = ((bf16[4,32,640]{2,1,0:T(8,128)(2,1)}), bf16[4,32,640]{2,1,0:T(8,128)(2,1)S(1)}, u32[]{:S(2)}, u32[]{:S(2)}) async-start(bf16[4,32,640]{2,1,0:T(8,128)(2,1)} %bitcast.21), calls=%async_computation.6 | async-start | bytes 327680 | tf_op jit(solution)/shard_map/all_to_all | solution.py:153
  384.2 0.6 broadcast_multiply_fusion
  384.8 0.7 broadcast_in_dim.107
  385.6 1.1 convert.9
  386.7 2.2 all-to-all-done.5
  388.9 4.8 %all-to-all-start.6 = ((bf16[4,32,640]{2,1,0:T(8,128)(2,1)}), bf16[4,32,640]{2,1,0:T(8,128)(2,1)S(1)}, u32[]{:S(2)}, u32[]{:S(2)}) async-start(bf16[4,32,640]{2,1,0:T(8,128)(2,1)} %bitcast.23), calls=%async_computation.7 | async-start | bytes 327680 | tf_op jit(solution)/shard_map/all_to_all | solution.py:156
  393.7 0.7 slice_bitcast_fusion
  394.5 0.7 broadcast_in_dim.108
  395.2 3.1 all-to-all-done.6
  398.4 0.7 broadcast_in_dim.109
  (61 shorter events, 3.1 us)
Async XLA Ops:
  7.2 143.6 %copy-start = (s32[1,4096]{1,0:T(1,128)S(1)}, s32[1,4096]{1,0:T(1,128)}, u32[]{:S(2)}) copy-start(s32[1,4096]{1,0:T(1,128)} %param.23) | copy-start | bytes 49156
  7.2 36.3 %copy-start.9 = (bf16[1,32,2560]{2,1,0:T(8,128)(2,1)S(1)}, bf16[1,32,2560]{2,1,0:T(8,128)(2,1)}, u32[]{:S(2)}) copy-start(bf16[1,32,2560]{2,1,0:T(8,128)(2,1)} %param.15) | copy-start | bytes 491524
  7.2 41.8 %copy-start.10 = (f32[2,5]{1,0:T(2,128)S(1)}, f32[2,5]{1,0:T(2,128)}, u32[]{:S(2)}) copy-start(f32[2,5]{1,0:T(2,128)} %param.20) | copy-start | bytes 124
  7.2 53.1 %all-gather.7.cloned.1.call-start = ((), (), s32[]{:S(2)}) async-start(), calls=%async_computation.9 | async-start | bytes 2785280 | tf_op jit(solution)/shard_map/all_gather | solution.py:104
  18.3 82.7 %all-gather.9.cloned.1.call-start = ((), (), s32[]{:S(2)}) async-start(), calls=%async_computation.10 | async-start | bytes 2785280 | tf_op jit(solution)/shard_map/all_gather | solution.py:105
  28.6 123.8 %all-gather.11.cloned.1.call-start = ((), (), s32[]{:S(2)}) async-start(), calls=%async_computation.13 | async-start | bytes 2785280 | tf_op jit(solution)/shard_map/all_gather | solution.py:162
  32.1 12.1 %all-to-all-start = ((bf16[32,4,640]{2,0,1:T(8,128)(2,1)}), bf16[32,4,640]{2,0,1:T(8,128)(2,1)S(1)}, u32[]{:S(2)}, u32[]{:S(2)}) async-start(bf16[32,4,640]{2,0,1:T(8,128)(2,1)} %copy.116), calls=%async_computation | async-start | bytes 327680 | tf_op jit(solution)/shard_map/all_to_all | solution.py:96
  36.8 152.2 %all-gather.13.cloned.1.call-start = ((), (), s32[]{:S(2)}) async-start(), calls=%async_computation.14 | async-start | bytes 2785280 | tf_op jit(solution)/shard_map/all_gather | solution.py:163
  44.2 9.5 %all-to-all-start.2 = ((bf16[32,4,640]{2,0,1:T(8,128)(2,1)}), bf16[32,4,640]{2,0,1:T(8,128)(2,1)S(1)}, u32[]{:S(2)}, u32[]{:S(2)}) async-start(bf16[32,4,640]{2,0,1:T(8,128)(2,1)} %copy.121), calls=%async_computation.2 | async-start | bytes 327680 | tf_op jit(solution)/shard_map/all_to_all | solution.py:99
  49.0 325.7 %reduce-scatter.3.cloned.1.call-start = ((), (), s32[]{:S(2)}) async-start(), calls=%async_computation.11 | async-start | bytes 11141120 | tf_op jit(solution)/shard_map/reduce_scatter | solution.py:131
  63.3 45.8 %copy-start.3 = (bf16[2048,640]{0,1:T(8,128)(2,1)}, bf16[2048,640]{0,1:T(8,128)(2,1)S(1)}, u32[]{:S(2)}) copy-start(bf16[2048,640]{0,1:T(8,128)(2,1)S(1)} %copy.118) | copy-start | bytes 7864324
  109.1 2.7 copy-start.4
  109.1 3.6 copy-start.7
  112.7 1.3 copy-start.5
  112.7 1.6 copy-start.6
  148.4 1.0 copy-start.8
  148.5 237.1 %reduce-scatter.5.cloned.1.call-start = ((), (), s32[]{:S(2)}) async-start(), calls=%async_computation.12 | async-start | bytes 11141120 | tf_op jit(solution)/shard_map/reduce_scatter | solution.py:193
  189.0 6.1 %slice-start = ((s8[10485760]{0:T(1024)(128)(4,1)}), s8[4194304]{0:T(1024)(128)(4,1)S(1)}, s32[]{:S(2)}) async-start(s8[10485760]{0:T(1024)(128)(4,1)} %bitcast.80), calls=%async_computation.15 | async-start | bytes 8388608
  189.0 7.3 %slice-start.1 = ((s8[10485760]{0:T(1024)(128)(4,1)}), s8[4194304]{0:T(1024)(128)(4,1)S(1)}, s32[]{:S(2)}) async-start(s8[10485760]{0:T(1024)(128)(4,1)} %bitcast.80), calls=%async_computation.16 | async-start | bytes 8388608
  189.0 7.9 %slice-start.2 = ((s8[10485760]{0:T(1024)(128)(4,1)}), s8[2097152]{0:T(1024)(128)(4,1)S(1)}, s32[]{:S(2)}) async-start(s8[10485760]{0:T(1024)(128)(4,1)} %bitcast.80), calls=%async_computation.17 | async-start | bytes 4194304
  198.6 4.0 copy-start.2
  236.9 162.3 %copy-start.1 = (s32[1,4096]{1,0:T(1,128)S(1)}, s32[1,4096]{1,0:T(1,128)}, u32[]{:S(2)}) copy-start(s32[1,4096]{1,0:T(1,128)} %param.23) | copy-start | bytes 49156
  369.9 9.5 %all-to-all-start.4 = ((bf16[4,32,640]{2,1,0:T(8,128)(2,1)}), bf16[4,32,640]{2,1,0:T(8,128)(2,1)S(1)}, u32[]{:S(2)}, u32[]{:S(2)}) async-start(bf16[4,32,640]{2,1,0:T(8,128)(2,1)} %convert_element_type.95), calls=%async_computation.4 | async-start | bytes 327680 | tf_op jit(solution)/shard_map/all_to_all | solution.py:146
  379.4 9.5 %all-to-all-start.5 = ((bf16[4,32,640]{2,1,0:T(8,128)(2,1)}), bf16[4,32,640]{2,1,0:T(8,128)(2,1)S(1)}, u32[]{:S(2)}, u32[]{:S(2)}) async-start(bf16[4,32,640]{2,1,0:T(8,128)(2,1)} %bitcast.21), calls=%async_computation.6 | async-start | bytes 327680 | tf_op jit(solution)/shard_map/all_to_all | solution.py:153
  388.9 9.5 %all-to-all-start.6 = ((bf16[4,32,640]{2,1,0:T(8,128)(2,1)}), bf16[4,32,640]{2,1,0:T(8,128)(2,1)S(1)}, u32[]{:S(2)}, u32[]{:S(2)}) async-start(bf16[4,32,640]{2,1,0:T(8,128)(2,1)} %bitcast.23), calls=%async_computation.7 | async-start | bytes 327680 | tf_op jit(solution)/shard_map/all_to_all | solution.py:156
Sparse Core Ops, SparseCore 0:
  18.5 41.7 all-gather.6
  62.1 38.8 all-gather.8
  103.4 41.4 all-gather.10
  147.0 41.9 all-gather.12
  191.4 73.8 reduce-scatter.2
  267.7 74.0 reduce-scatter.4
where the time goes:
time: 408 us; the launch traced here: 406 us
  blocking collectives  149 us (37%)
  waiting for transfers between devices  83.5 us (20%)
  local copies, waits for them, and re-layouts  52.1 us (13%)
  matrix products  50.7 us (12%)
  other arithmetic  32.3 us (8%)
  starting transfers between devices  24.2 us (6%)
  between operations  14.4 us (4%)
    psum x1, blocking collectives, local(): slope_grad = lax.psum(slope_local, ('seq', 'dp')) / patch_total  129 us
    all_gather x1, waiting for transfers between devices, local(): lax.all_gather(local_values, 'seq', axis=0, tiled=True)  37.8 us
    all_gather x1, waiting for transfers between devices, local(): lax.all_gather(memory_values[0], 'seq', axis=0, tiled=True)  27.1 us
    another operation x4, local copies, waits for them, and re-layouts, key_terms(): jnp.stack([key_grad.reshape(row_count, -1), value_grad.reshape(row_count,...  23.7 us
    another operation x2, other arithmetic, key_terms(): jnp.stack([key_grad.reshape(row_count, -1), value_grad.reshape(row_count,...  17.5 us
    dot_general x2, matrix products, key_terms(): jnp.einsum('chrk,crhs->khs', softmax_b, grad_rows, preferred_element_type...  15.4 us
    unnamed x33, local copies, waits for them, and re-layouts  10.6 us
    all_to_all x1, blocking collectives, local(): lax.all_to_all(self_keys[0], 'head', split_axis=1, concat_axis=0, tiled=T...  10 us
  transfers between devices with their start and end apart: 11, of which 7 were waited for; matrix products, arithmetic and copies ran while one was open for 31% of the time, Pallas kernels for 0%

commit v1 on v0

--- a/solution.py
+++ b/solution.py
@@ -157,7 +157,7 @@
             self_dv.astype(jnp.bfloat16), "head", split_axis=0, concat_axis=1, tiled=True
         ),
     )
-    slope_grad = lax.psum(slope_local, ("seq", "dp")) / patch_total
+    slope_grad = lax.psum(lax.psum(slope_local, "seq"), "dp") / patch_total
     memory_all_keys, memory_all_values = (
         lax.all_gather(memory_keys[0], "seq", axis=0, tiled=True),
         lax.all_gather(memory_values[0], "seq", axis=0, tiled=True),

time: 408 us -> 362 us (0.89)
  blocking collectives: 149 us -> 55.9 us
  waiting for transfers between devices: 83.5 us -> 130 us
    psum x1 -> x2, blocking collectives: 129 us -> 36.7 us  [local(): slope_grad = lax.psum(lax.psum(slope_local, 'seq'), 'dp') / patch_total]
    reduce_scatter x1, waiting for transfers between devices: 0.01 us -> 48.7 us  [local(): lax.psum_scatter(key_terms(text_ds_b, text_p_b, text_query_blocks, text_g...]
  transfers between devices with their start and end apart: 11 -> 11, of which waited for: 7 -> 7; matrix products, arithmetic and copies ran while one was open for 31% -> 35% of each run, Pallas kernels for 0% -> 0%
where the time goes in v1:
time: 362 us; the launch traced here: 360 us
  waiting for transfers between devices  130 us (36%)
  blocking collectives  55.9 us (15%)
  local copies, waits for them, and re-layouts  52.2 us (14%)
  matrix products  50.7 us (14%)
  other arithmetic  32.3 us (9%)
  starting transfers between devices  24.3 us (7%)
  between operations  14.4 us (4%)
    reduce_scatter x1, waiting for transfers between devices, local(): lax.psum_scatter(key_terms(text_ds_b, text_p_b, text_query_blocks, text_g...  48.7 us
    all_gather x1, waiting for transfers between devices, local(): lax.all_gather(local_values, 'seq', axis=0, tiled=True)  37.8 us
    psum x2, blocking collectives, local(): slope_grad = lax.psum(lax.psum(slope_local, 'seq'), 'dp') / patch_total  36.7 us
    all_gather x1, waiting for transfers between devices, local(): lax.all_gather(memory_values[0], 'seq', axis=0, tiled=True)  27.1 us
    another operation x4, local copies, waits for them, and re-layouts, key_terms(): jnp.stack([key_grad.reshape(row_count, -1), value_grad.reshape(row_count,...  23.7 us
    another operation x2, other arithmetic, key_terms(): jnp.stack([key_grad.reshape(row_count, -1), value_grad.reshape(row_count,...  17.5 us
    dot_general x2, matrix products, key_terms(): jnp.einsum('chrk,crhs->khs', softmax_b, grad_rows, preferred_element_type...  15.4 us
    unnamed x33, local copies, waits for them, and re-layouts  10.6 us
  transfers between devices with their start and end apart: 11, of which 7 were waited for; matrix products, arithmetic and copies ran while one was open for 35% of the time, Pallas kernels for 0%

profile of v1, /device:TPU:2, one launch (start us, length us, event | category | flops | bytes accessed | tf_op | source)
XLA Modules:
  0.0 359.8 jit_solution(12420908455035417592)
XLA Ops:
  7.3 1.0 all_to_all.85
  8.3 10.0 %all_to_all.109 = bf16[32,4,640]{2,0,1:T(8,128)(2,1)} all-to-all(bf16[32,4,640]{2,0,1:T(8,128)(2,1)S(1)} %copy.117), channel_id=1, replica_groups=mesh['seq'=16,'head'=4,'dp'=4] {'head'}, dimensions={1} | all-to-all | bytes 327680 | tf_op jit(solution)/shard_map/all_to_all | solution.py:97
  18.4 1.0 all_to_all.92
  19.4 9.2 %all_to_all.110 = bf16[32,4,640]{2,0,1:T(8,128)(2,1)} all-to-all(bf16[32,4,640]{2,0,1:T(8,128)(2,1)S(1)} %copy.122), channel_id=1, replica_groups=mesh['seq'=16,'head'=4,'dp'=4] {'head'}, dimensions={1} | all-to-all | bytes 327680 | tf_op jit(solution)/shard_map/all_to_all | solution.py:98
  28.6 1.7 copy.136
  30.4 1.0 all_to_all.82
  31.4 0.7 copy.116
  32.1 4.7 %all-to-all-start = ((bf16[32,4,640]{2,0,1:T(8,128)(2,1)}), bf16[32,4,640]{2,0,1:T(8,128)(2,1)S(1)}, u32[]{:S(2)}, u32[]{:S(2)}) async-start(bf16[32,4,640]{2,0,1:T(8,128)(2,1)} %copy.116), calls=%async_computation | async-start | bytes 327680 | tf_op jit(solution)/shard_map/all_to_all | solution.py:96
  36.8 1.7 copy.140
  38.6 0.8 reduce-window.4
  39.4 0.7 fusion.25
  40.2 0.8 select_reduce_fusion.1
  41.4 1.8 abs_convert_fusion
  43.5 0.7 copy.121
  44.2 4.8 %all-to-all-start.2 = ((bf16[32,4,640]{2,0,1:T(8,128)(2,1)}), bf16[32,4,640]{2,0,1:T(8,128)(2,1)S(1)}, u32[]{:S(2)}, u32[]{:S(2)}) async-start(bf16[32,4,640]{2,0,1:T(8,128)(2,1)} %copy.121), calls=%async_computation.2 | async-start | bytes 327680 | tf_op jit(solution)/shard_map/all_to_all | solution.py:99
  49.4 4.3 %all-to-all-done.2 = bf16[32,4,640]{2,0,1:T(8,128)(2,1)S(1)} async-done(((bf16[32,4,640]{2,0,1:T(8,128)(2,1)}), bf16[32,4,640]{2,0,1:T(8,128)(2,1)S(1)}, u32[]{:S(2)}, u32[]{:S(2)}) %all-to-all-start.2) | async-done | bytes 163872 | tf_op jit(solution)/shard_map/all_to_all | solution.py:99
  54.1 6.2 %all-gather.7.cloned.1.call-done = bf16[2048,640]{1,0:T(8,128)(2,1)} async-done(((bf16[128,640]{1,0:T(8,128)(2,1)}), bf16[2048,640]{1,0:T(8,128)(2,1)}) %all-gather.7.cloned.1.call-update) | async-done | bytes 2621456 | tf_op jit(solution)/shard_map/all_gather | solution.py:104
  60.3 3.0 copy.118
  63.3 37.8 %all-gather.9.cloned.1.call-done = bf16[2048,640]{1,0:T(8,128)(2,1)} async-done(((bf16[128,640]{1,0:T(8,128)(2,1)}), bf16[2048,640]{1,0:T(8,128)(2,1)}) %all-gather.9.cloned.1.call-update) | async-done | bytes 2621456 | tf_op jit(solution)/shard_map/all_gather | solution.py:105
  101.0 4.5 %copy.123 = bf16[2048,640]{0,1:T(8,128)(2,1)} copy(bf16[2048,640]{1,0:T(8,128)(2,1)} %all-gather.9.cloned.1.call-done) | data formatting | bytes 5242880 | tf_op jit(solution)/shard_map/all_gather | solution.py:105
  105.5 3.6 select_add_fusion
  109.2 1.6 fusion.28
  110.8 1.0 copy-done.4
  111.8 1.0 copy-done.7
  112.8 1.3 multiply_reduce_fusion.3
  114.3 2.4 multiply_reduce_fusion.2
  116.7 3.2 convolution_multiply_fusion
  119.9 6.0 %copy.131 = f32[2048,1,640]{2,0,1:T(8,128)} copy(f32[2048,1,640]{0,2,1:T(8,128)} %bitcast.79) | data formatting | bytes 10485760 | tf_op jit(solution)/shard_map/stack;reshape | solution.py:77
  125.9 8.0 %fusion.7 = f32[5,2048,128]{1,2,0:T(8,128)} fusion(bf16[128,5,128]{0,2,1:T(8,128)(2,1)S(1)} %copy.130, f32[5,128]{1,0:T(8,128)S(1)} %get-tuple-element.85, f32[5,128,2048]{2,1,0:T(8,128)} %copy-done.4), kind=kOutput, calls=%fused_computation.22 | convolution fusion | flops 339479168 | bytes 10652160 | tf_op jit(solution)/shard_map/chrk,crhs->khs/dot_general | solution.py:74
  133.8 5.9 %copy.132 = f32[2048,1,640]{2,0,1:T(8,128)} copy(f32[2048,1,640]{0,2,1:T(8,128)} %bitcast.84) | data formatting | bytes 10485760 | tf_op jit(solution)/shard_map/stack;reshape | solution.py:77
  139.7 8.8 %pad_maximum_fusion = f32[2048,2,640]{2,0,1:T(8,128)} fusion(f32[2048,1,640]{2,0,1:T(8,128)} %copy.132, f32[2048,1,640]{2,0,1:T(8,128)} %copy.131), kind=kLoop, calls=%fused_computation.2 | loop fusion | flops 2621440 | bytes 20971520 | tf_op jit(solution)/shard_map/stack | solution.py:77
  148.8 0.7 copy-done.8
  149.7 1.1 copy.139
  150.8 1.6 compare_select_fusion
  152.4 9.5 %fusion.29 = (f32[5,256]{1,0:T(8,128)S(1)}, f32[5,256,2048]{2,1,0:T(8,128)}) fusion(f32[256,2048]{1,0:T(8,128)} %compare_select_fusion, bf16[256,5,128]{0,2,1:T(8,128)(2,1)S(1)} %bitcast.87, bf16[2048,5,128]{0,2,1:T(8,128)(2,1)} %bitcast.104), kind=kOutput, calls=%fused_computation.62 | convolution fusion | flops 681576448 | bytes 15537152 | tf_op jit(solution)/shard_map/while/body/eval_jaxpr/sub | solution.py:44
  161.9 27.1 %all-gather.13.cloned.1.call-done = bf16[1,2048,640]{1,2,0:T(8,128)(2,1)} async-done(((bf16[1,128,640]{1,2,0:T(8,128)(2,1)}), bf16[1,2048,640]{1,2,0:T(8,128)(2,1)}) %all-gather.13.cloned.1.call-update) | async-done | bytes 2621456 | tf_op jit(solution)/shard_map/all_gather | solution.py:163
  189.0 6.1 %multiply_reduce_fusion = (f32[5,256]{1,0:T(8,128)S(1)}, f32[5,256,2048]{2,1,0:T(8,128)S(1)}) fusion(f32[5,256,2048]{2,1,0:T(8,128)} %get-tuple-element.90, f32[5,256]{1,0:T(8,128)S(1)} %get-tuple-element.89, bf16[256,5,128]{0,2,1:T(8,128)(2,1)S(1)} %bitcast.96, bf16[2048,5,128]{0,2,1:T(8,128)(2,1)} %bitcast.106), kind=kOutput, calls=%fused_computation.5 | convolution fusion | flops 678951680 | bytes 23930880 | tf_op jit(solution)/shard_map/while/body/eval_jaxpr/rhs,khs->hrk/dot_general | solution.py:48
  195.1 1.1 slice-done.1
  196.2 0.6 slice-done.2
  196.8 1.8 multiply_convert_fusion
  198.6 3.9 %convolution_multiply_fusion.1 = f32[5,2048,128]{1,2,0:T(8,128)} fusion(bf16[256,5,128]{0,2,1:T(8,128)(2,1)S(1)} %bitcast.88, bf16[5,256,2048]{2,1,0:T(8,128)(2,1)S(1)} %multiply_convert_fusion), kind=kOutput, calls=%fused_computation.21 | convolution fusion | flops 672399360 | bytes 10813440 | tf_op jit(solution)/shard_map/chrk,crhs->khs/dot_general | solution.py:71
  202.6 5.9 %copy.143 = f32[2048,1,640]{2,0,1:T(8,128)} copy(f32[2048,1,640]{0,2,1:T(8,128)} %bitcast.78) | data formatting | bytes 10485760 | tf_op jit(solution)/shard_map/stack;reshape | solution.py:77
  208.5 7.4 %fusion.3 = f32[5,2048,128]{1,2,0:T(8,128)} fusion(bf16[256,5,128]{0,2,1:T(8,128)(2,1)S(1)} %bitcast.97, f32[5,256,2048]{2,1,0:T(8,128)} %get-tuple-element.90, f32[5,256]{1,0:T(8,128)S(1)} %get-tuple-element.89), kind=kOutput, calls=%fused_computation.9 | convolution fusion | flops 676331520 | bytes 16061440 | tf_op jit(solution)/shard_map/chrk,crhs->khs/dot_general | solution.py:74
  215.9 5.9 %copy.144 = f32[2048,1,640]{2,0,1:T(8,128)} copy(f32[2048,1,640]{0,2,1:T(8,128)} %bitcast.85) | data formatting | bytes 10485760 | tf_op jit(solution)/shard_map/stack;reshape | solution.py:77
  221.9 8.7 %pad_maximum_fusion.1 = f32[2048,2,640]{2,0,1:T(8,128)} fusion(f32[2048,1,640]{2,0,1:T(8,128)} %copy.144, f32[2048,1,640]{2,0,1:T(8,128)} %copy.143), kind=kLoop, calls=%fused_computation.3 | loop fusion | flops 2621440 | bytes 20971520 | tf_op jit(solution)/shard_map/stack | solution.py:77
  230.6 5.3 %fusion.14 = bf16[5,256,128]{1,2,0:T(8,128)(2,1)S(1)} fusion(bf16[5,256,2048]{2,1,0:T(8,128)(2,1)} %copy-done.2, bf16[2048,5,128]{0,2,1:T(8,128)(2,1)} %bitcast.105), kind=kOutput, calls=%fused_computation.31 | convolution fusion | flops 671416320 | bytes 8192000 | tf_op jit(solution)/shard_map/while/body/eval_jaxpr/hrk,khs->rhs/dot_general | solution.py:55
  235.9 26.1 %psum.14 = f32[2,5]{1,0:T(2,128)S(1)} all-reduce(f32[2,5]{1,0:T(2,128)S(1)} %maximum_negate_fusion), channel_id=1, replica_groups=mesh['seq'=16,'head'=4,'dp'=4] {'seq'}, use_global_device_ids=true, to_apply=%region_10.11 | all-reduce | flops 10 | bytes 80 | tf_op jit(solution)/shard_map/psum | solution.py:160
  262.1 0.9 copy.145
  263.0 10.6 %psum.15 = f32[2,5]{1,0:T(2,128)S(1)} all-reduce(f32[2,5]{1,0:T(2,128)S(1)} %psum.14), channel_id=1, replica_groups=mesh['seq'=16,'head'=4,'dp'=4] {'dp'}, use_global_device_ids=true, to_apply=%region_11.12 | all-reduce | flops 10 | bytes 80 | tf_op jit(solution)/shard_map/psum | solution.py:160
  273.5 2.6 fusion.21
  276.2 0.9 convert_element_type.95
  277.1 4.8 %all-to-all-start.4 = ((bf16[4,32,640]{2,1,0:T(8,128)(2,1)}), bf16[4,32,640]{2,1,0:T(8,128)(2,1)S(1)}, u32[]{:S(2)}, u32[]{:S(2)}) async-start(bf16[4,32,640]{2,1,0:T(8,128)(2,1)} %convert_element_type.95), calls=%async_computation.4 | async-start | bytes 327680 | tf_op jit(solution)/shard_map/all_to_all | solution.py:146
  281.9 1.1 convert.8
  283.0 0.8 fusion.27
  283.8 2.8 all-to-all-done.4
  286.6 4.8 %all-to-all-start.5 = ((bf16[4,32,640]{2,1,0:T(8,128)(2,1)}), bf16[4,32,640]{2,1,0:T(8,128)(2,1)S(1)}, u32[]{:S(2)}, u32[]{:S(2)}) async-start(bf16[4,32,640]{2,1,0:T(8,128)(2,1)} %bitcast.21), calls=%async_computation.6 | async-start | bytes 327680 | tf_op jit(solution)/shard_map/all_to_all | solution.py:153
  292.0 0.7 broadcast_in_dim.107
  292.8 48.7 %reduce-scatter.5.cloned.1.call-done = f32[128,2,640]{2,0,1:T(8,128)} async-done(((f32[2048,2,640]{2,0,1:T(8,128)}), f32[128,2,640]{2,0,1:T(8,128)}) %reduce-scatter.5.cloned.1.call-update) | async-done | bytes 655376 | tf_op jit(solution)/shard_map/reduce_scatter | solution.py:193
  341.5 1.1 convert.9
  342.6 4.8 %all-to-all-start.6 = ((bf16[4,32,640]{2,1,0:T(8,128)(2,1)}), bf16[4,32,640]{2,1,0:T(8,128)(2,1)S(1)}, u32[]{:S(2)}, u32[]{:S(2)}) async-start(bf16[4,32,640]{2,1,0:T(8,128)(2,1)} %bitcast.23), calls=%async_computation.7 | async-start | bytes 327680 | tf_op jit(solution)/shard_map/all_to_all | solution.py:156
  347.4 0.7 slice_bitcast_fusion
  348.3 0.7 broadcast_in_dim.108
  349.0 3.1 all-to-all-done.6
  352.2 0.7 broadcast_in_dim.109
  (62 shorter events, 3.7 us)
Async XLA Ops:
  7.2 143.6 %copy-start = (s32[1,4096]{1,0:T(1,128)S(1)}, s32[1,4096]{1,0:T(1,128)}, u32[]{:S(2)}) copy-start(s32[1,4096]{1,0:T(1,128)} %param.23) | copy-start | bytes 49156
  7.2 36.2 %copy-start.9 = (bf16[1,32,2560]{2,1,0:T(8,128)(2,1)S(1)}, bf16[1,32,2560]{2,1,0:T(8,128)(2,1)}, u32[]{:S(2)}) copy-start(bf16[1,32,2560]{2,1,0:T(8,128)(2,1)} %param.15) | copy-start | bytes 491524
  7.2 41.8 %copy-start.10 = (f32[2,5]{1,0:T(2,128)S(1)}, f32[2,5]{1,0:T(2,128)}, u32[]{:S(2)}) copy-start(f32[2,5]{1,0:T(2,128)} %param.20) | copy-start | bytes 124
  7.2 53.1 %all-gather.7.cloned.1.call-start = ((), (), s32[]{:S(2)}) async-start(), calls=%async_computation.9 | async-start | bytes 2785280 | tf_op jit(solution)/shard_map/all_gather | solution.py:104
  18.3 82.7 %all-gather.9.cloned.1.call-start = ((), (), s32[]{:S(2)}) async-start(), calls=%async_computation.10 | async-start | bytes 2785280 | tf_op jit(solution)/shard_map/all_gather | solution.py:105
  28.6 123.8 %all-gather.11.cloned.1.call-start = ((), (), s32[]{:S(2)}) async-start(), calls=%async_computation.13 | async-start | bytes 2785280 | tf_op jit(solution)/shard_map/all_gather | solution.py:162
  32.1 12.1 %all-to-all-start = ((bf16[32,4,640]{2,0,1:T(8,128)(2,1)}), bf16[32,4,640]{2,0,1:T(8,128)(2,1)S(1)}, u32[]{:S(2)}, u32[]{:S(2)}) async-start(bf16[32,4,640]{2,0,1:T(8,128)(2,1)} %copy.116), calls=%async_computation | async-start | bytes 327680 | tf_op jit(solution)/shard_map/all_to_all | solution.py:96
  36.8 152.1 %all-gather.13.cloned.1.call-start = ((), (), s32[]{:S(2)}) async-start(), calls=%async_computation.14 | async-start | bytes 2785280 | tf_op jit(solution)/shard_map/all_gather | solution.py:163
  44.2 9.5 %all-to-all-start.2 = ((bf16[32,4,640]{2,0,1:T(8,128)(2,1)}), bf16[32,4,640]{2,0,1:T(8,128)(2,1)S(1)}, u32[]{:S(2)}, u32[]{:S(2)}) async-start(bf16[32,4,640]{2,0,1:T(8,128)(2,1)} %copy.121), calls=%async_computation.2 | async-start | bytes 327680 | tf_op jit(solution)/shard_map/all_to_all | solution.py:99
  49.0 233.0 %reduce-scatter.3.cloned.1.call-start = ((), (), s32[]{:S(2)}) async-start(), calls=%async_computation.11 | async-start | bytes 11141120 | tf_op jit(solution)/shard_map/reduce_scatter | solution.py:131
  63.3 45.9 %copy-start.3 = (bf16[2048,640]{0,1:T(8,128)(2,1)}, bf16[2048,640]{0,1:T(8,128)(2,1)S(1)}, u32[]{:S(2)}) copy-start(bf16[2048,640]{0,1:T(8,128)(2,1)S(1)} %copy.118) | copy-start | bytes 7864324
  109.1 2.7 copy-start.4
  109.1 3.6 %copy-start.7 = (bf16[2048,640]{0,1:T(8,128)(2,1)S(1)}, bf16[2048,640]{0,1:T(8,128)(2,1)}, u32[]{:S(2)}) copy-start(bf16[2048,640]{0,1:T(8,128)(2,1)} %copy.123) | copy-start | bytes 7864324
  112.8 1.3 copy-start.5
  112.8 1.6 copy-start.6
  148.5 1.0 copy-start.8
  148.5 193.0 %reduce-scatter.5.cloned.1.call-start = ((), (), s32[]{:S(2)}) async-start(), calls=%async_computation.12 | async-start | bytes 11141120 | tf_op jit(solution)/shard_map/reduce_scatter | solution.py:193
  189.0 6.1 %slice-start = ((s8[10485760]{0:T(1024)(128)(4,1)}), s8[4194304]{0:T(1024)(128)(4,1)S(1)}, s32[]{:S(2)}) async-start(s8[10485760]{0:T(1024)(128)(4,1)} %bitcast.80), calls=%async_computation.15 | async-start | bytes 8388608
  189.0 7.3 %slice-start.1 = ((s8[10485760]{0:T(1024)(128)(4,1)}), s8[4194304]{0:T(1024)(128)(4,1)S(1)}, s32[]{:S(2)}) async-start(s8[10485760]{0:T(1024)(128)(4,1)} %bitcast.80), calls=%async_computation.16 | async-start | bytes 8388608
  189.0 7.9 %slice-start.2 = ((s8[10485760]{0:T(1024)(128)(4,1)}), s8[2097152]{0:T(1024)(128)(4,1)S(1)}, s32[]{:S(2)}) async-start(s8[10485760]{0:T(1024)(128)(4,1)} %bitcast.80), calls=%async_computation.17 | async-start | bytes 4194304
  198.6 4.0 %copy-start.2 = (bf16[5,256,2048]{2,1,0:T(8,128)(2,1)}, bf16[5,256,2048]{2,1,0:T(8,128)(2,1)S(1)}, u32[]{:S(2)}) copy-start(bf16[5,256,2048]{2,1,0:T(8,128)(2,1)S(1)} %multiply_convert_fusion) | copy-start | bytes 15728644
  263.0 90.0 %copy-start.1 = (s32[1,4096]{1,0:T(1,128)S(1)}, s32[1,4096]{1,0:T(1,128)}, u32[]{:S(2)}) copy-start(s32[1,4096]{1,0:T(1,128)} %param.23) | copy-start | bytes 49156
  277.1 9.5 %all-to-all-start.4 = ((bf16[4,32,640]{2,1,0:T(8,128)(2,1)}), bf16[4,32,640]{2,1,0:T(8,128)(2,1)S(1)}, u32[]{:S(2)}, u32[]{:S(2)}) async-start(bf16[4,32,640]{2,1,0:T(8,128)(2,1)} %convert_element_type.95), calls=%async_computation.4 | async-start | bytes 327680 | tf_op jit(solution)/shard_map/all_to_all | solution.py:146
  286.6 56.0 %all-to-all-start.5 = ((bf16[4,32,640]{2,1,0:T(8,128)(2,1)}), bf16[4,32,640]{2,1,0:T(8,128)(2,1)S(1)}, u32[]{:S(2)}, u32[]{:S(2)}) async-start(bf16[4,32,640]{2,1,0:T(8,128)(2,1)} %bitcast.21), calls=%async_computation.6 | async-start | bytes 327680 | tf_op jit(solution)/shard_map/all_to_all | solution.py:153
  342.6 9.5 %all-to-all-start.6 = ((bf16[4,32,640]{2,1,0:T(8,128)(2,1)}), bf16[4,32,640]{2,1,0:T(8,128)(2,1)S(1)}, u32[]{:S(2)}, u32[]{:S(2)}) async-start(bf16[4,32,640]{2,1,0:T(8,128)(2,1)} %bitcast.23), calls=%async_computation.7 | async-start | bytes 327680 | tf_op jit(solution)/shard_map/all_to_all | solution.py:156
Sparse Core Ops, SparseCore 0:
  18.4 41.7 all-gather.6
  62.1 38.8 all-gather.8
  103.4 41.4 all-gather.10
  147.0 41.9 all-gather.12
  191.4 73.6 reduce-scatter.2
  267.5 73.9 reduce-scatter.4
